TPU v7x, 32 devices: a whole 2x2x4 slice. The times are simulated.
32 devices in a mesh: pole: 2 (over y), prow: 1, pcol: 16 (over z, x, core).
Axes of the slice: x: 2, y: 2, z: 4, core: 2. Of those that a mesh axis runs over, the one named last changes fastest.
Arguments:
- anc_inverse: float32 [12288, 6144], P(('pole', 'prow'), 'pcol'), parts along dimension 0, may hold values from -8 to 8
- anc_factor: float32 [12288, 768], P(('pole', 'pcol')), parts along dimension 0, may hold values from -0.078125 to 0.078125
- win_factor: float32 [1536, 768], P('pole'), parts along dimension 0, may hold values from -0.375 to 0.375
- pivot_inverse: float32 [6, 256, 256], P('pole'), parts along dimension 0, may hold values from -6 to 6
- structure: int32 [3, 24], replicated, may hold values 0 or 1
Outputs:
- anc_columns: float32 [12288, 768], P(('pole', 'prow', 'pcol')), parts along dimension 0
- win_inverse: float32 [1536, 768], P('pole'), parts along dimension 0
There are 2 independent parts, one for each index of `pole`. A program takes and returns all parts, laid end to end along the dimension named above; an argument that names none is the same for every part. Nothing has to cross between parts.
All inputs are finite; a program needn't handle non-finite values.
Results may differ from a plain program's by a relative error of at most 0.0001.
Values sent between devices are 32-bit elements; how exact they have to be, the bound alone decides.
A program may use at most 128 MiB of HBM per device.

v0:
```python
import jax
import jax.numpy as jnp
from jax import lax
from jax.sharding import PartitionSpec as P

precise = lax.Precision.HIGHEST


def product(left, right):
    return jnp.dot(left, right, precision=precise, preferred_element_type=jnp.float32)


def on_device(anc_inverse, anc_factor, win_factor, pivot_inverse, structure):
    row_count = lax.axis_size("prow")
    col_count = lax.axis_size("pcol")
    row_index = lax.axis_index("prow")
    col_index = lax.axis_index("pcol")
    block_rows = anc_inverse.shape[0]
    block_cols = anc_inverse.shape[1]
    steps_total = pivot_inverse.shape[0]
    width = pivot_inverse.shape[1]
    all_cols = anc_factor.shape[1]
    block_count = structure.shape[1]
    ratio_cols = col_count // row_count
    share_rows = block_rows // col_count
    structure_cols = structure.T.astype(jnp.float32)
    global_rows = col_index * block_cols + lax.iota(jnp.int32, block_cols)
    onehot_rows = (
        (global_rows // width)[:, None] == lax.iota(jnp.int32, block_count)[None, :]
    ).astype(jnp.float32)
    kept_rows = product(onehot_rows, structure_cols)
    share_offset = col_index * share_rows
    share_global = (row_index * col_count + col_index) * share_rows + lax.iota(
        jnp.int32, share_rows
    )
    onehot_share = (
        (share_global // width)[:, None] == lax.iota(jnp.int32, block_count)[None, :]
    ).astype(jnp.float32)
    kept_share = product(onehot_share, structure_cols)
    slot_ids = lax.iota(jnp.int32, col_count)
    source_flag = (slot_ids // row_count == col_index - row_index * ratio_cols).astype(jnp.float32)
    pieces = jnp.tile(anc_factor.reshape(row_count, share_rows, all_cols), (ratio_cols, 1, 1))
    outgoing = pieces * source_flag[:, None, None]
    incoming = lax.all_to_all(outgoing, "pcol", split_axis=0, concat_axis=0, tiled=True)
    factor_share = jnp.sum(incoming, axis=0)
    column_store = {}
    share_store = {}
    window_blocks = {}
    for k in range(steps_total - 1, -1, -1):
        first_col = k * width
        factor_now = anc_factor[:, first_col : first_col + width] * kept_rows[:, k : k + 1]
        share_factor = factor_share[:, first_col : first_col + width] * kept_share[:, k : k + 1]
        finished = list(range(k + 1, steps_total))
        if finished:
            stacked = jnp.concatenate([column_store[j] for j in finished], axis=1)
            factor_win = win_factor[first_col + width :, first_col : first_col + width]

        def term_rows(start, count, factor_now=factor_now):
            return product(anc_inverse, factor_now)

        share_image = lax.psum_scatter(
            term_rows(jnp.int32(0), share_rows * lax.axis_size("pcol")),
            "pcol",
            scatter_dimension=0,
            tiled=True,
        )
        if finished:
            share_image = share_image + product(
                lax.dynamic_slice_in_dim(stacked, share_offset, share_rows, 0), factor_win
            )
        share_column = -share_image
        column_now = lax.all_gather(share_column, "pcol", axis=0, tiled=True)
        crossings = [product(share_store[j].T, share_factor) for j in finished]
        pivot_part = product(share_factor.T, share_column)
        cross_sums = []
        if finished:
            cross_total = lax.psum(jnp.stack(crossings), ("prow", "pcol"))
            cross_sums = [cross_total[position] for position in range(len(finished))]
        pivot_sum = lax.psum(pivot_part, ("prow", "pcol"))
        for position, j in enumerate(finished):
            running = cross_sums[position]
            for i in finished:
                running = running + product(
                    window_blocks[j, i],
                    win_factor[i * width : (i + 1) * width, first_col : first_col + width],
                )
            window_blocks[j, k] = -running
            window_blocks[k, j] = -running.T
        pivot_block = pivot_inverse[k] - pivot_sum
        for j in finished:
            pivot_block = pivot_block - product(
                win_factor[j * width : (j + 1) * width, first_col : first_col + width].T,
                window_blocks[j, k],
            )
        window_blocks[k, k] = pivot_block
        column_store[k] = column_now
        share_store[k] = share_column
    anc_columns = jnp.concatenate([share_store[k] for k in range(steps_total)], axis=1)
    win_inverse = jnp.concatenate(
        [
            jnp.concatenate([window_blocks[i, k] for k in range(steps_total)], axis=1)
            for i in range(steps_total)
        ],
        axis=0,
    )
    return (anc_columns, win_inverse)


def solution(mesh):
    in_specs = (
        P(("pole", "prow"), "pcol"),
        P(("pole", "pcol"), None),
        P("pole", None),
        P("pole", None, None),
        P(),
    )
    out_specs = (P(("pole", "prow", "pcol"), None), P("pole", None))
    return jax.shard_map(
        on_device, mesh=mesh, in_specs=in_specs, out_specs=out_specs, check_vma=False
    )
```

profile of v0, /device:TPU:0, one launch (start us, length us, event | category | flops | bytes accessed | tf_op | source)
XLA Modules:
  0.0 905.3 jit_solution(14524148858973868540)
XLA Ops:
  7.2 1.0 fusion.40
  8.2 19.4 %convolution_bitcast_fusion = f32[6144,256]{0,1:T(8,128)} fusion(f32[6144,384]{1,0:T(8,128)} %param.5, f32[384,768]{1,0:T(8,128)} %param.6, f32[384]{0:T(512)S(1)} %get-tuple-element.7), kind=kOutput, calls=%fused_computation.3 | convolution fusion | flops 7247855616 | bytes 16123392 | tf_op jit(solution)/shard_map/dot_general | solution.py:10
  27.9 1.0 copy-done.2
  28.9 19.2 %convolution_bitcast_fusion.1 = f32[6144,256]{0,1:T(8,128)} fusion(f32[6144,384]{1,0:T(8,128)} %param.5, f32[384,768]{1,0:T(8,128)S(1)} %copy-done.2, f32[384]{0:T(512)S(1)} %get-tuple-element.8), kind=kOutput, calls=%fused_computation.4 | convolution fusion | flops 7247855616 | bytes 16123904 | tf_op jit(solution)/shard_map/dot_general | solution.py:10
  48.1 8.4 broadcast_multiply_fusion
  56.5 7.4 all-to-all-start
  63.9 346.9 %reduce-scatter.8.cloned.1.call-done = f32[384,256]{0,1:T(8,128)} async-done(((f32[6144,256]{0,1:T(8,128)}), f32[384,256]{0,1:T(8,128)}) %reduce-scatter.8.cloned.1.call-update) | async-done | bytes 393232 | tf_op jit(solution)/shard_map/reduce_scatter | solution.py:61
  410.8 1.8 neg.30
  412.9 19.2 %convolution_bitcast_fusion.2 = f32[6144,256]{0,1:T(8,128)} fusion(f32[6144,384]{1,0:T(8,128)} %param.5, f32[384,768]{1,0:T(8,128)S(1)} %copy-done.2, f32[384]{0:T(512)S(1)} %get-tuple-element.6), kind=kOutput, calls=%fused_computation.5 | convolution fusion | flops 7247855616 | bytes 16123904 | tf_op jit(solution)/shard_map/dot_general | solution.py:10
  432.2 121.9 %reduce-scatter.6.cloned.1.call-done = f32[384,256]{0,1:T(8,128)} async-done(((f32[6144,256]{0,1:T(8,128)}), f32[384,256]{0,1:T(8,128)}) %reduce-scatter.6.cloned.1.call-update) | async-done | bytes 393232 | tf_op jit(solution)/shard_map/reduce_scatter | solution.py:61
  554.1 64.0 %all-gather.3.cloned.1.call-done = f32[6144,256]{0,1:T(8,128)} async-done(((f32[384,256]{0,1:T(8,128)}), f32[6144,256]{0,1:T(8,128)}) %all-gather.3.cloned.1.call-update) | async-done | bytes 6291472 | tf_op jit(solution)/shard_map/all_gather | solution.py:72
  618.1 2.6 fusion.1
  621.0 84.6 %reduce-scatter.4.cloned.1.call-done = f32[384,256]{0,1:T(8,128)} async-done(((f32[6144,256]{0,1:T(8,128)}), f32[384,256]{0,1:T(8,128)}) %reduce-scatter.4.cloned.1.call-update) | async-done | bytes 393232 | tf_op jit(solution)/shard_map/reduce_scatter | solution.py:61
  705.7 64.0 %all-gather.5.cloned.1.call-done = f32[6144,256]{0,1:T(8,128)} async-done(((f32[384,256]{0,1:T(8,128)}), f32[6144,256]{0,1:T(8,128)}) %all-gather.5.cloned.1.call-update) | async-done | bytes 6291472 | tf_op jit(solution)/shard_map/all_gather | solution.py:72
  769.7 2.4 fusion
  772.1 7.7 reduce_sum.9
  779.8 0.9 convolution_bitcast_fusion.7
  780.7 1.4 fusion.20
  782.1 1.6 fusion.21
  783.7 0.9 convolution_bitcast_fusion.6
  785.4 1.4 fusion.19
  786.8 1.6 fusion.11
  788.4 0.8 copy.42
  789.3 1.4 copy.32
  790.7 93.1 %all-reduce.3.cloned.1.call-done = (f32[256,256]{1,0:T(8,128)}, f32[256,256]{1,0:T(8,128)}, f32[2,256,256]{1,2,0:T(8,128)}, f32[256,256]{0,1:T(8,128)}, f32[256,256]{1,0:T(8,128)}) async-done(((f32[256,256]{1,0:T(8,128)}, f32[256,256]{1,0:T(8,128)}, f32[2,256,256]{1,2,0:T(8,128)}, f32[256,256]{0,1:T(8,128)}, f32[256,256]{1,0:T(8,128)}), (f32[256,256]{1,0:T(8,128)}, f32[256,256]{1,0:T(8,128)}, ...) | async-done | bytes 1572880 | tf_op jit(solution)/shard_map/psum | solution.py:79
  883.8 1.1 bitcast_subtract_fusion
  884.9 1.4 fusion.7
  886.3 1.6 convolution_add_fusion.3
  888.0 1.5 fusion.6
  892.9 1.7 fusion.4
  894.6 1.3 fusion.2
  896.9 1.6 maximum_maximum_fusion
  (47 shorter events, 6.4 us)
Async XLA Ops:
  7.2 403.7 %reduce-scatter.8.cloned.1.call-start = ((), (), s32[]{:S(2)}) async-start(), calls=%async_computation.6 | async-start | bytes 6684672 | tf_op jit(solution)/shard_map/reduce_scatter | solution.py:61
  27.6 1.3 copy-start.2
  27.6 526.5 %reduce-scatter.6.cloned.1.call-start = ((), (), s32[]{:S(2)}) async-start(), calls=%async_computation.5 | async-start | bytes 6684672 | tf_op jit(solution)/shard_map/reduce_scatter | solution.py:61
  56.5 715.6 %all-to-all-start = ((f32[16,384,768]{2,1,0:T(8,128)}), f32[16,384,768]{2,1,0:T(8,128)}, u32[]{:S(2)}, u32[]{:S(2)}) async-start(f32[16,384,768]{2,1,0:T(8,128)} %broadcast_multiply_fusion), calls=%async_computation.3 | async-start | bytes 37748736 | tf_op jit(solution)/shard_map/all_to_all | solution.py:44
  63.9 554.3 %all-gather.3.cloned.1.call-start = ((), (), s32[]{:S(2)}) async-start(), calls=%async_computation.7 | async-start | bytes 6684672 | tf_op jit(solution)/shard_map/all_gather | solution.py:72
  412.6 293.1 %reduce-scatter.4.cloned.1.call-start = ((), (), s32[]{:S(2)}) async-start(), calls=%async_computation.4 | async-start | bytes 6684672 | tf_op jit(solution)/shard_map/reduce_scatter | solution.py:61
  432.1 337.5 %all-gather.5.cloned.1.call-start = ((), (), s32[]{:S(2)}) async-start(), calls=%async_computation.8 | async-start | bytes 6684672 | tf_op jit(solution)/shard_map/all_gather | solution.py:72
  620.7 263.0 %all-reduce.3.cloned.1.call-start = ((), (), s32[]{:S(2)}) async-start(), calls=%async_computation.9 | async-start | bytes 3145728 | tf_op jit(solution)/shard_map/psum | solution.py:79
  772.1 7.7 copy-start
  779.8 3.9 copy-start.1
  785.4 3.0 slice-start
  785.4 3.8 copy-start.3
  790.7 97.3 %copy-start.4 = (f32[768,768]{1,0:T(8,128)S(1)}, f32[768,768]{1,0:T(8,128)}, u32[]{:S(2)}) copy-start(f32[768,768]{1,0:T(8,128)} %param.7) | copy-start | bytes 7077892
  790.7 97.3 %copy-start.7 = (f32[1,256,256]{1,2,0:T(8,128)S(1)}, f32[1,256,256]{1,2,0:T(8,128)}, u32[]{:S(2)}) copy-start(f32[1,256,256]{1,2,0:T(8,128)} %copy.42) | copy-start | bytes 786436
  883.8 6.5 copy-start.10
  889.5 0.7 copy-start.5
  892.9 3.0 copy-start.6
  895.9 0.9 copy-start.8
  895.9 1.0 copy-start.9
Sparse Core Ops, SparseCore 0:
  27.8 383.0 reduce-scatter.7
  415.3 138.7 reduce-scatter.5
  557.0 61.1 all-gather.2
  621.9 83.6 reduce-scatter.3
  708.7 60.9 all-gather.4
  788.5 95.2 all-reduce.2
where the time goes:
time: 906 us; the launch traced here: 905 us
  waiting for transfers between devices  775 us (86%)
  matrix products  80.8 us (9%)
  other arithmetic  21.5 us (2%)
  between operations  14.3 us (2%)
    reduce_scatter x3, waiting for transfers between devices, on_device(): lax.psum_scatter(term_rows(jnp.int32(0), share_rows * lax.axis_size('pcol...  553 us
    all_gather x2, waiting for transfers between devices, on_device(): column_now = lax.all_gather(share_column, 'pcol', axis=0, tiled=True)  128 us
    psum x1, waiting for transfers between devices, on_device(): pivot_sum = lax.psum(pivot_part, ('prow', 'pcol'))  93.1 us
    dot_general x20, matrix products, product(): jnp.dot(left, right, precision=precise, preferred_element_type=jnp.float32)  80.8 us
  transfers between devices with their start and end apart: 7, of which 6 were waited for; matrix products, arithmetic and copies ran while one was open for 6% of the time, Pallas kernels for 0%

commit v1 on v0

--- a/solution.py
+++ b/solution.py
@@ -4,6 +4,19 @@
 from jax.sharding import PartitionSpec as P
 
 precise = lax.Precision.HIGHEST
+
+
+def ring_gather(x, axis, dim):
+    ways = lax.axis_size(axis)
+    up = [(d, (d + 1) % ways) for d in range(ways)]
+    down = [(d, (d - 1) % ways) for d in range(ways)]
+    earlier, later = ([x], [x])
+    for _ in range(ways // 2):
+        earlier.append(lax.ppermute(earlier[-1], axis, up))
+    for _ in range((ways - 1) // 2):
+        later.append(lax.ppermute(later[-1], axis, down))
+    line = jnp.concatenate([*earlier[::-1], *later[1:]], axis=dim)
+    return jnp.roll(line, (lax.axis_index(axis) - ways // 2) * x.shape[dim], axis=dim)
 
 
 def product(left, right):
@@ -69,7 +82,7 @@
                 lax.dynamic_slice_in_dim(stacked, share_offset, share_rows, 0), factor_win
             )
         share_column = -share_image
-        column_now = lax.all_gather(share_column, "pcol", axis=0, tiled=True)
+        column_now = ring_gather(share_column, "pcol", 0)
         crossings = [product(share_store[j].T, share_factor) for j in finished]
         pivot_part = product(share_factor.T, share_column)
         cross_sums = []

time: 906 us -> 865 us (0.955)
  waiting for transfers between devices: 775 us -> 483 us
  starting transfers between devices: 8.28 us -> 218 us
  local copies, waits for them, and re-layouts: 5.82 us -> 22.5 us
  other arithmetic: 21.5 us -> 37.6 us
    reduce_scatter x3, waiting for transfers between devices: 553 us -> 312 us  [on_device(): lax.psum_scatter(term_rows(jnp.int32(0), share_rows * lax.axis_size('pcol...]
    ppermute x0 -> x30, starting transfers between devices: none -> 210 us  [the longest x16 166 us: ring_gather(): earlier.append(lax.ppermute(earlier[-1], axis, up))]
    all_gather x2 -> x0, waiting for transfers between devices: 128 us -> none  [on_device(): column_now = lax.all_gather(share_column, 'pcol', axis=0, tiled=True)]
    ppermute x0 -> x30, waiting for transfers between devices: none -> 68.3 us  [the longest x16 49.6 us: ring_gather(): earlier.append(lax.ppermute(earlier[-1], axis, up))]
    unnamed x24 -> x55, local copies, waits for them, and re-layouts: 4.68 us -> 21.2 us
    concatenate x0 -> x2, other arithmetic: none -> 14.7 us  [ring_gather(): jnp.roll(line, (lax.axis_index(axis) - ways // 2) * x.shape[dim], axis=dim)]
    psum x1, waiting for transfers between devices: 93.1 us -> 103 us  [on_device(): pivot_sum = lax.psum(pivot_part, ('prow', 'pcol'))]
  transfers between devices with their start and end apart: 7 -> 35, of which waited for: 6 -> 20; matrix products, arithmetic and copies ran while one was open for 6% -> 12% of each run, Pallas kernels for 0% -> 0%
where the time goes in v1:
time: 865 us; the launch traced here: 858 us
  waiting for transfers between devices  483 us (56%)
  starting transfers between devices  218 us (25%)
  matrix products  82.9 us (10%)
  other arithmetic  37.6 us (4%)
  local copies, waits for them, and re-layouts  22.5 us (3%)
  between operations  14.6 us (2%)
    reduce_scatter x3, waiting for transfers between devices, on_device(): lax.psum_scatter(term_rows(jnp.int32(0), share_rows * lax.axis_size('pcol...  312 us
    ppermute x16, starting transfers between devices, ring_gather(): earlier.append(lax.ppermute(earlier[-1], axis, up))  166 us
    psum x1, waiting for transfers between devices, on_device(): pivot_sum = lax.psum(pivot_part, ('prow', 'pcol'))  103 us
    dot_general x20, matrix products, product(): jnp.dot(left, right, precision=precise, preferred_element_type=jnp.float32)  82.9 us
    ppermute x16, waiting for transfers between devices, ring_gather(): earlier.append(lax.ppermute(earlier[-1], axis, up))  49.6 us
    ppermute x14, starting transfers between devices, ring_gather(): later.append(lax.ppermute(later[-1], axis, down))  44.2 us
    unnamed x55, local copies, waits for them, and re-layouts  21.2 us
    ppermute x14, waiting for transfers between devices, ring_gather(): later.append(lax.ppermute(later[-1], axis, down))  18.6 us
  transfers between devices with their start and end apart: 35, of which 20 were waited for; matrix products, arithmetic and copies ran while one was open for 12% of the time, Pallas kernels for 0%

profile of v1, /device:TPU:0, one launch (start us, length us, event | category | flops | bytes accessed | tf_op | source)
XLA Modules:
  0.0 858.3 jit_solution(8340731472737733266)
XLA Ops:
  7.2 9.7 %broadcast_multiply_fusion = f32[16,384,768]{2,1,0:T(8,128)} fusion(f32[16]{0:T(128)S(1)} %compare_convert_fusion, f32[384,768]{1,0:T(8,128)} %param.8), kind=kLoop, calls=%fused_computation.8 | loop fusion | flops 4718592 | bytes 20054080 | tf_op jit(solution)/shard_map/mul | solution.py:56
  16.9 7.5 all-to-all-start
  24.9 19.2 %convolution_bitcast_fusion = f32[6144,256]{0,1:T(8,128)} fusion(f32[6144,384]{1,0:T(8,128)} %param.7, f32[384,768]{1,0:T(8,128)S(1)} %copy-done.1, f32[384]{0:T(512)S(1)} %get-tuple-element.8), kind=kOutput, calls=%fused_computation.9 | convolution fusion | flops 7247855616 | bytes 16123904 | tf_op jit(solution)/shard_map/dot_general | solution.py:23
  44.3 19.2 %convolution_bitcast_fusion.1 = f32[6144,256]{0,1:T(8,128)} fusion(f32[6144,384]{1,0:T(8,128)} %param.7, f32[384,768]{1,0:T(8,128)S(1)} %copy-done.1, f32[384]{0:T(512)S(1)} %get-tuple-element.9), kind=kOutput, calls=%fused_computation.10 | convolution fusion | flops 7247855616 | bytes 16123904 | tf_op jit(solution)/shard_map/dot_general | solution.py:23
  63.6 311.7 %reduce-scatter.8.cloned.1.call-done = f32[384,256]{0,1:T(8,128)} async-done(((f32[6144,256]{0,1:T(8,128)}), f32[384,256]{0,1:T(8,128)}) %reduce-scatter.8.cloned.1.call-update) | async-done | bytes 393232 | tf_op jit(solution)/shard_map/reduce_scatter | solution.py:74
  376.5 9.9 %collective-permute-done = f32[384,256]{0,1:T(8,128)S(1)} collective-permute-done((f32[384,256]{0,1:T(8,128)S(1)}, f32[384,256]{0,1:T(8,128)S(1)}, u32[]{:S(2)}, u32[]{:S(2)}) %collective-permute-start) | collective-permute-done | bytes 393248 | tf_op jit(solution)/shard_map/ppermute | solution.py:15
  390.9 5.7 collective-permute-done.1
  401.0 5.7 collective-permute-done.2
  406.6 12.3 %collective-permute-start.3 = (f32[384,256]{0,1:T(8,128)S(1)}, f32[384,256]{0,1:T(8,128)S(1)}, u32[]{:S(2)}, u32[]{:S(2)}) collective-permute-start(f32[384,256]{0,1:T(8,128)S(1)} %collective-permute-done.2), channel_id=1, source_target_pairs={{0,1},{1,2},{2,3},{3,4},{4,5},{5,6},{6,7},{7,8},{8,9},{9,10},{10,1... | collective-permute-start | bytes 1179656 | tf_op jit(solution)/shard_map/ppermute | solution.py:15
  421.3 11.2 %collective-permute-done.3 = f32[384,256]{0,1:T(8,128)S(1)} collective-permute-done((f32[384,256]{0,1:T(8,128)S(1)}, f32[384,256]{0,1:T(8,128)S(1)}, u32[]{:S(2)}, u32[]{:S(2)}) %collective-permute-start.3) | collective-permute-done | bytes 393248 | tf_op jit(solution)/shard_map/ppermute | solution.py:15
  432.5 8.9 %collective-permute-start.4 = (f32[384,256]{0,1:T(8,128)S(1)}, f32[384,256]{0,1:T(8,128)S(1)}, u32[]{:S(2)}, u32[]{:S(2)}) collective-permute-start(f32[384,256]{0,1:T(8,128)S(1)} %collective-permute-done.3), channel_id=1, source_target_pairs={{0,1},{1,2},{2,3},{3,4},{4,5},{5,6},{6,7},{7,8},{8,9},{9,10},{10,1... | collective-permute-start | bytes 1179656 | tf_op jit(solution)/shard_map/ppermute | solution.py:15
  443.3 5.7 collective-permute-done.4
  449.0 6.2 collective-permute-start.5
  458.8 4.7 collective-permute-done.5
  465.4 19.2 %convolution_bitcast_fusion.2 = f32[6144,256]{0,1:T(8,128)} fusion(f32[6144,384]{1,0:T(8,128)} %param.7, f32[384,768]{1,0:T(8,128)S(1)} %copy-done.1, f32[384]{0:T(512)S(1)} %get-tuple-element.7), kind=kOutput, calls=%fused_computation.11 | convolution fusion | flops 7247855616 | bytes 16123904 | tf_op jit(solution)/shard_map/dot_general | solution.py:23
  484.7 9.9 %collective-permute-start.13 = (f32[384,256]{0,1:T(8,128)}, f32[384,256]{0,1:T(8,128)}, u32[]{:S(2)}, u32[]{:S(2)}) collective-permute-start(f32[384,256]{0,1:T(8,128)} %collective-permute-done.12), channel_id=1, source_target_pairs={{0,15},{1,0},{2,1},{3,2},{4,3},{5,4},{6,5},{7,6},{8,7},{9,8},{10,9... | collective-permute-start | bytes 1179656 | tf_op jit(solution)/shard_map/ppermute | solution.py:17
  494.6 58.4 %collective-permute-start.7 = (f32[384,256]{0,1:T(8,128)}, f32[384,256]{0,1:T(8,128)}, u32[]{:S(2)}, u32[]{:S(2)}) collective-permute-start(f32[384,256]{0,1:T(8,128)} %collective-permute-done.6), channel_id=1, source_target_pairs={{0,1},{1,2},{2,3},{3,4},{4,5},{5,6},{6,7},{7,8},{8,9},{9,10},{10,1... | collective-permute-start | bytes 1179656 | tf_op jit(solution)/shard_map/ppermute | solution.py:15
  576.8 14.2 %collective-permute-start.15 = (f32[384,256]{0,1:T(8,128)S(1)}, f32[384,256]{0,1:T(8,128)S(1)}, u32[]{:S(2)}, u32[]{:S(2)}) collective-permute-start(f32[384,256]{0,1:T(8,128)S(1)} %fusion.3), channel_id=1, source_target_pairs={{0,1},{1,2},{2,3},{3,4},{4,5},{5,6},{6,7},{7,8},{8,9},{9,10},{10,1... | collective-permute-start | bytes 1179656 | tf_op jit(solution)/shard_map/ppermute | solution.py:15
  592.3 10.1 %collective-permute-start.16 = (f32[384,256]{0,1:T(8,128)S(1)}, f32[384,256]{0,1:T(8,128)S(1)}, u32[]{:S(2)}, u32[]{:S(2)}) collective-permute-start(f32[384,256]{0,1:T(8,128)S(1)} %collective-permute-done.15), channel_id=1, source_target_pairs={{0,1},{1,2},{2,3},{3,4},{4,5},{5,6},{6,7},{7,8},{8,9},{9,10},{10,1... | collective-permute-start | bytes 1179656 | tf_op jit(solution)/shard_map/ppermute | solution.py:15
  605.8 18.7 %collective-permute-start.17 = (f32[384,256]{0,1:T(8,128)S(1)}, f32[384,256]{0,1:T(8,128)S(1)}, u32[]{:S(2)}, u32[]{:S(2)}) collective-permute-start(f32[384,256]{0,1:T(8,128)S(1)} %collective-permute-done.16), channel_id=1, source_target_pairs={{0,1},{1,2},{2,3},{3,4},{4,5},{5,6},{6,7},{7,8},{8,9},{9,10},{10,1... | collective-permute-start | bytes 1179656 | tf_op jit(solution)/shard_map/ppermute | solution.py:15
  625.9 15.3 %collective-permute-start.18 = (f32[384,256]{0,1:T(8,128)S(1)}, f32[384,256]{0,1:T(8,128)S(1)}, u32[]{:S(2)}, u32[]{:S(2)}) collective-permute-start(f32[384,256]{0,1:T(8,128)S(1)} %collective-permute-done.17), channel_id=1, source_target_pairs={{0,1},{1,2},{2,3},{3,4},{4,5},{5,6},{6,7},{7,8},{8,9},{9,10},{10,1... | collective-permute-start | bytes 1179656 | tf_op jit(solution)/shard_map/ppermute | solution.py:15
  642.5 9.3 %collective-permute-start.19 = (f32[384,256]{0,1:T(8,128)S(1)}, f32[384,256]{0,1:T(8,128)S(1)}, u32[]{:S(2)}, u32[]{:S(2)}) collective-permute-start(f32[384,256]{0,1:T(8,128)S(1)} %collective-permute-done.18), channel_id=1, source_target_pairs={{0,1},{1,2},{2,3},{3,4},{4,5},{5,6},{6,7},{7,8},{8,9},{9,10},{10,1... | collective-permute-start | bytes 1179656 | tf_op jit(solution)/shard_map/ppermute | solution.py:15
  655.1 4.6 collective-permute-start.26
  665.0 4.7 collective-permute-start.27
  669.7 7.0 collective-permute-start.21
  676.7 6.5 collective-permute-done.27
  683.1 4.6 collective-permute-start.28
  688.0 8.8 %fusion.1 = f32[6144,256]{0,1:T(8,128)} fusion(s32[]{:T(128)S(6)} %select_n.37, f32[6144,256]{0,1:T(8,128)} %constant_dynamic-update-slice_fusion), kind=kLoop, calls=%fused_computation.13 | loop fusion | flops 1572864 | bytes 12582916 | tf_op jit(solution)/shard_map/jit(_roll_dynamic)/concatenate | solution.py:19
  702.0 4.6 collective-permute-done.29
  706.6 5.9 fusion
  714.9 7.6 reduce_sum.9
  732.8 102.6 %all-reduce.3.cloned.1.call-done = (f32[256,256]{1,0:T(8,128)}, f32[256,256]{1,0:T(8,128)}, f32[2,256,256]{1,2,0:T(8,128)}, f32[256,256]{0,1:T(8,128)}, f32[256,256]{1,0:T(8,128)}) async-done(((f32[256,256]{1,0:T(8,128)}, f32[256,256]{1,0:T(8,128)}, f32[2,256,256]{1,2,0:T(8,128)}, f32[256,256]{0,1:T(8,128)}, f32[256,256]{1,0:T(8,128)}), (f32[256,256]{1,0:T(8,128)}, f32[256,256]{1,0:T(8,128)}, ...) | async-done | bytes 1572880 | tf_op jit(solution)/shard_map/psum | solution.py:92
  (137 shorter events, 94.1 us)
Async XLA Ops:
  16.9 698.0 %all-to-all-start = ((f32[16,384,768]{2,1,0:T(8,128)}), f32[16,384,768]{2,1,0:T(8,128)}, u32[]{:S(2)}, u32[]{:S(2)}) async-start(f32[16,384,768]{2,1,0:T(8,128)} %broadcast_multiply_fusion), calls=%async_computation.3 | async-start | bytes 37748736 | tf_op jit(solution)/shard_map/all_to_all | solution.py:57
  24.5 350.9 %reduce-scatter.8.cloned.1.call-start = ((), (), s32[]{:S(2)}) async-start(), calls=%async_computation.6 | async-start | bytes 6684672 | tf_op jit(solution)/shard_map/reduce_scatter | solution.py:74
  44.1 530.5 %reduce-scatter.6.cloned.1.call-start = ((), (), s32[]{:S(2)}) async-start(), calls=%async_computation.5 | async-start | bytes 6684672 | tf_op jit(solution)/shard_map/reduce_scatter | solution.py:74
  63.6 648.9 %reduce-scatter.4.cloned.1.call-start = ((), (), s32[]{:S(2)}) async-start(), calls=%async_computation.4 | async-start | bytes 6684672 | tf_op jit(solution)/shard_map/reduce_scatter | solution.py:74
  376.4 10.1 %collective-permute-start = (f32[384,256]{0,1:T(8,128)S(1)}, f32[384,256]{0,1:T(8,128)S(1)}, u32[]{:S(2)}, u32[]{:S(2)}) collective-permute-start(f32[384,256]{0,1:T(8,128)S(1)} %neg.30), channel_id=1, source_target_pairs={{0,1},{1,2},{2,3},{3,4},{4,5},{5,6},{6,7},{7,8},{8,9},{9,10},{10,1... | collective-permute-start | bytes 1179656 | tf_op jit(solution)/shard_map/ppermute | solution.py:15
  386.4 10.1 %collective-permute-start.1 = (f32[384,256]{0,1:T(8,128)S(1)}, f32[384,256]{0,1:T(8,128)S(1)}, u32[]{:S(2)}, u32[]{:S(2)}) collective-permute-start(f32[384,256]{0,1:T(8,128)S(1)} %collective-permute-done), channel_id=1, source_target_pairs={{0,1},{1,2},{2,3},{3,4},{4,5},{5,6},{6,7},{7,8},{8,9},{9,10},{10,1... | collective-permute-start | bytes 1179656 | tf_op jit(solution)/shard_map/ppermute | solution.py:15
  386.4 10.1 %collective-permute-start.8 = (f32[384,256]{0,1:T(8,128)S(1)}, f32[384,256]{0,1:T(8,128)S(1)}, u32[]{:S(2)}, u32[]{:S(2)}) collective-permute-start(f32[384,256]{0,1:T(8,128)S(1)} %neg.30), channel_id=1, source_target_pairs={{0,15},{1,0},{2,1},{3,2},{4,3},{5,4},{6,5},{7,6},{8,7},{9,8},{10,9... | collective-permute-start | bytes 1179656 | tf_op jit(solution)/shard_map/ppermute | solution.py:17
  396.5 10.1 %collective-permute-start.2 = (f32[384,256]{0,1:T(8,128)S(1)}, f32[384,256]{0,1:T(8,128)S(1)}, u32[]{:S(2)}, u32[]{:S(2)}) collective-permute-start(f32[384,256]{0,1:T(8,128)S(1)} %collective-permute-done.1), channel_id=1, source_target_pairs={{0,1},{1,2},{2,3},{3,4},{4,5},{5,6},{6,7},{7,8},{8,9},{9,10},{10,1... | collective-permute-start | bytes 1179656 | tf_op jit(solution)/shard_map/ppermute | solution.py:15
  396.5 22.4 %collective-permute-start.9 = (f32[384,256]{0,1:T(8,128)S(1)}, f32[384,256]{0,1:T(8,128)S(1)}, u32[]{:S(2)}, u32[]{:S(2)}) collective-permute-start(f32[384,256]{0,1:T(8,128)S(1)} %collective-permute-done.8), channel_id=1, source_target_pairs={{0,15},{1,0},{2,1},{3,2},{4,3},{5,4},{6,5},{7,6},{8,7},{9,8},{10,9... | collective-permute-start | bytes 1179656 | tf_op jit(solution)/shard_map/ppermute | solution.py:17
  406.6 25.9 %collective-permute-start.3 = (f32[384,256]{0,1:T(8,128)S(1)}, f32[384,256]{0,1:T(8,128)S(1)}, u32[]{:S(2)}, u32[]{:S(2)}) collective-permute-start(f32[384,256]{0,1:T(8,128)S(1)} %collective-permute-done.2), channel_id=1, source_target_pairs={{0,1},{1,2},{2,3},{3,4},{4,5},{5,6},{6,7},{7,8},{8,9},{9,10},{10,1... | collective-permute-start | bytes 1179656 | tf_op jit(solution)/shard_map/ppermute | solution.py:15
  419.0 22.4 %collective-permute-start.10 = (f32[384,256]{0,1:T(8,128)S(1)}, f32[384,256]{0,1:T(8,128)S(1)}, u32[]{:S(2)}, u32[]{:S(2)}) collective-permute-start(f32[384,256]{0,1:T(8,128)S(1)} %collective-permute-done.9), channel_id=1, source_target_pairs={{0,15},{1,0},{2,1},{3,2},{4,3},{5,4},{6,5},{7,6},{8,7},{9,8},{10,9... | collective-permute-start | bytes 1179656 | tf_op jit(solution)/shard_map/ppermute | solution.py:17
  432.5 16.5 %collective-permute-start.4 = (f32[384,256]{0,1:T(8,128)S(1)}, f32[384,256]{0,1:T(8,128)S(1)}, u32[]{:S(2)}, u32[]{:S(2)}) collective-permute-start(f32[384,256]{0,1:T(8,128)S(1)} %collective-permute-done.3), channel_id=1, source_target_pairs={{0,1},{1,2},{2,3},{3,4},{4,5},{5,6},{6,7},{7,8},{8,9},{9,10},{10,1... | collective-permute-start | bytes 1179656 | tf_op jit(solution)/shard_map/ppermute | solution.py:15
  442.1 13.1 %collective-permute-start.11 = (f32[384,256]{0,1:T(8,128)S(1)}, f32[384,256]{0,1:T(8,128)}, u32[]{:S(2)}, u32[]{:S(2)}) collective-permute-start(f32[384,256]{0,1:T(8,128)S(1)} %collective-permute-done.10), channel_id=1, source_target_pairs={{0,15},{1,0},{2,1},{3,2},{4,3},{5,4},{6,5},{7,6},{8,7},{9,8},{10,9... | collective-permute-start | bytes 1179656 | tf_op jit(solution)/shard_map/ppermute | solution.py:17
  449.0 14.4 %collective-permute-start.5 = (f32[384,256]{0,1:T(8,128)S(1)}, f32[384,256]{0,1:T(8,128)}, u32[]{:S(2)}, u32[]{:S(2)}) collective-permute-start(f32[384,256]{0,1:T(8,128)S(1)} %collective-permute-done.4), channel_id=1, source_target_pairs={{0,1},{1,2},{2,3},{3,4},{4,5},{5,6},{6,7},{7,8},{8,9},{9,10},{10,1... | collective-permute-start | bytes 1179656 | tf_op jit(solution)/shard_map/ppermute | solution.py:15
  455.2 29.5 %collective-permute-start.12 = (f32[384,256]{0,1:T(8,128)}, f32[384,256]{0,1:T(8,128)}, u32[]{:S(2)}, u32[]{:S(2)}) collective-permute-start(f32[384,256]{0,1:T(8,128)} %collective-permute-done.11), channel_id=1, source_target_pairs={{0,15},{1,0},{2,1},{3,2},{4,3},{5,4},{6,5},{7,6},{8,7},{9,8},{10,9... | collective-permute-start | bytes 1179656 | tf_op jit(solution)/shard_map/ppermute | solution.py:17
  463.5 31.1 %collective-permute-start.6 = (f32[384,256]{0,1:T(8,128)}, f32[384,256]{0,1:T(8,128)}, u32[]{:S(2)}, u32[]{:S(2)}) collective-permute-start(f32[384,256]{0,1:T(8,128)} %collective-permute-done.5), channel_id=1, source_target_pairs={{0,1},{1,2},{2,3},{3,4},{4,5},{5,6},{6,7},{7,8},{8,9},{9,10},{10,1... | collective-permute-start | bytes 1179656 | tf_op jit(solution)/shard_map/ppermute | solution.py:15
  484.7 350.6 %all-reduce.3.cloned.1.call-start = ((), (), s32[]{:S(2)}) async-start(), calls=%async_computation.7 | async-start | bytes 3145728 | tf_op jit(solution)/shard_map/psum | solution.py:92
  484.7 69.5 %collective-permute-start.13 = (f32[384,256]{0,1:T(8,128)}, f32[384,256]{0,1:T(8,128)}, u32[]{:S(2)}, u32[]{:S(2)}) collective-permute-start(f32[384,256]{0,1:T(8,128)} %collective-permute-done.12), channel_id=1, source_target_pairs={{0,15},{1,0},{2,1},{3,2},{4,3},{5,4},{6,5},{7,6},{8,7},{9,8},{10,9... | collective-permute-start | bytes 1179656 | tf_op jit(solution)/shard_map/ppermute | solution.py:17
  494.6 60.1 %collective-permute-start.7 = (f32[384,256]{0,1:T(8,128)}, f32[384,256]{0,1:T(8,128)}, u32[]{:S(2)}, u32[]{:S(2)}) collective-permute-start(f32[384,256]{0,1:T(8,128)} %collective-permute-done.6), channel_id=1, source_target_pairs={{0,1},{1,2},{2,3},{3,4},{4,5},{5,6},{6,7},{7,8},{8,9},{9,10},{10,1... | collective-permute-start | bytes 1179656 | tf_op jit(solution)/shard_map/ppermute | solution.py:15
  554.3 19.6 %collective-permute-start.14 = (f32[384,256]{0,1:T(8,128)}, f32[384,256]{0,1:T(8,128)S(1)}, u32[]{:S(2)}, u32[]{:S(2)}) collective-permute-start(f32[384,256]{0,1:T(8,128)} %collective-permute-done.13), channel_id=1, source_target_pairs={{0,15},{1,0},{2,1},{3,2},{4,3},{5,4},{6,5},{7,6},{8,7},{9,8},{10,9... | collective-permute-start | bytes 1179656 | tf_op jit(solution)/shard_map/ppermute | solution.py:17
  576.8 15.5 %collective-permute-start.15 = (f32[384,256]{0,1:T(8,128)S(1)}, f32[384,256]{0,1:T(8,128)S(1)}, u32[]{:S(2)}, u32[]{:S(2)}) collective-permute-start(f32[384,256]{0,1:T(8,128)S(1)} %fusion.3), channel_id=1, source_target_pairs={{0,1},{1,2},{2,3},{3,4},{4,5},{5,6},{6,7},{7,8},{8,9},{9,10},{10,1... | collective-permute-start | bytes 1179656 | tf_op jit(solution)/shard_map/ppermute | solution.py:15
  592.3 13.5 %collective-permute-start.16 = (f32[384,256]{0,1:T(8,128)S(1)}, f32[384,256]{0,1:T(8,128)S(1)}, u32[]{:S(2)}, u32[]{:S(2)}) collective-permute-start(f32[384,256]{0,1:T(8,128)S(1)} %collective-permute-done.15), channel_id=1, source_target_pairs={{0,1},{1,2},{2,3},{3,4},{4,5},{5,6},{6,7},{7,8},{8,9},{9,10},{10,1... | collective-permute-start | bytes 1179656 | tf_op jit(solution)/shard_map/ppermute | solution.py:15
  602.4 22.1 %collective-permute-start.23 = (f32[384,256]{0,1:T(8,128)S(1)}, f32[384,256]{0,1:T(8,128)S(1)}, u32[]{:S(2)}, u32[]{:S(2)}) collective-permute-start(f32[384,256]{0,1:T(8,128)S(1)} %fusion.3), channel_id=1, source_target_pairs={{0,15},{1,0},{2,1},{3,2},{4,3},{5,4},{6,5},{7,6},{8,7},{9,8},{10,9... | collective-permute-start | bytes 1179656 | tf_op jit(solution)/shard_map/ppermute | solution.py:17
  605.8 20.1 %collective-permute-start.17 = (f32[384,256]{0,1:T(8,128)S(1)}, f32[384,256]{0,1:T(8,128)S(1)}, u32[]{:S(2)}, u32[]{:S(2)}) collective-permute-start(f32[384,256]{0,1:T(8,128)S(1)} %collective-permute-done.16), channel_id=1, source_target_pairs={{0,1},{1,2},{2,3},{3,4},{4,5},{5,6},{6,7},{7,8},{8,9},{9,10},{10,1... | collective-permute-start | bytes 1179656 | tf_op jit(solution)/shard_map/ppermute | solution.py:15
  624.5 17.9 %collective-permute-start.24 = (f32[384,256]{0,1:T(8,128)S(1)}, f32[384,256]{0,1:T(8,128)S(1)}, u32[]{:S(2)}, u32[]{:S(2)}) collective-permute-start(f32[384,256]{0,1:T(8,128)S(1)} %collective-permute-done.23), channel_id=1, source_target_pairs={{0,15},{1,0},{2,1},{3,2},{4,3},{5,4},{6,5},{7,6},{8,7},{9,8},{10,9... | collective-permute-start | bytes 1179656 | tf_op jit(solution)/shard_map/ppermute | solution.py:17
  625.9 16.7 %collective-permute-start.18 = (f32[384,256]{0,1:T(8,128)S(1)}, f32[384,256]{0,1:T(8,128)S(1)}, u32[]{:S(2)}, u32[]{:S(2)}) collective-permute-start(f32[384,256]{0,1:T(8,128)S(1)} %collective-permute-done.17), channel_id=1, source_target_pairs={{0,1},{1,2},{2,3},{3,4},{4,5},{5,6},{6,7},{7,8},{8,9},{9,10},{10,1... | collective-permute-start | bytes 1179656 | tf_op jit(solution)/shard_map/ppermute | solution.py:15
  642.4 12.7 %collective-permute-start.25 = (f32[384,256]{0,1:T(8,128)S(1)}, f32[384,256]{0,1:T(8,128)S(1)}, u32[]{:S(2)}, u32[]{:S(2)}) collective-permute-start(f32[384,256]{0,1:T(8,128)S(1)} %collective-permute-done.24), channel_id=1, source_target_pairs={{0,15},{1,0},{2,1},{3,2},{4,3},{5,4},{6,5},{7,6},{8,7},{9,8},{10,9... | collective-permute-start | bytes 1179656 | tf_op jit(solution)/shard_map/ppermute | solution.py:17
  642.5 17.2 %collective-permute-start.19 = (f32[384,256]{0,1:T(8,128)S(1)}, f32[384,256]{0,1:T(8,128)S(1)}, u32[]{:S(2)}, u32[]{:S(2)}) collective-permute-start(f32[384,256]{0,1:T(8,128)S(1)} %collective-permute-done.18), channel_id=1, source_target_pairs={{0,1},{1,2},{2,3},{3,4},{4,5},{5,6},{6,7},{7,8},{8,9},{9,10},{10,1... | collective-permute-start | bytes 1179656 | tf_op jit(solution)/shard_map/ppermute | solution.py:15
  665.0 18.2 %collective-permute-start.27 = (f32[384,256]{0,1:T(8,128)S(1)}, f32[384,256]{0,1:T(8,128)S(1)}, u32[]{:S(2)}, u32[]{:S(2)}) collective-permute-start(f32[384,256]{0,1:T(8,128)S(1)} %collective-permute-done.26), channel_id=1, source_target_pairs={{0,15},{1,0},{2,1},{3,2},{4,3},{5,4},{6,5},{7,6},{8,7},{9,8},{10,9... | collective-permute-start | bytes 1179656 | tf_op jit(solution)/shard_map/ppermute | solution.py:17
  669.7 18.3 %collective-permute-start.21 = (f32[384,256]{0,1:T(8,128)S(1)}, f32[384,256]{0,1:T(8,128)S(1)}, u32[]{:S(2)}, u32[]{:S(2)}) collective-permute-start(f32[384,256]{0,1:T(8,128)S(1)} %collective-permute-done.20), channel_id=1, source_target_pairs={{0,1},{1,2},{2,3},{3,4},{4,5},{5,6},{6,7},{7,8},{8,9},{9,10},{10,1... | collective-permute-start | bytes 1179656 | tf_op jit(solution)/shard_map/ppermute | solution.py:15
  683.1 13.7 %collective-permute-start.28 = (f32[384,256]{0,1:T(8,128)S(1)}, f32[384,256]{0,1:T(8,128)S(1)}, u32[]{:S(2)}, u32[]{:S(2)}) collective-permute-start(f32[384,256]{0,1:T(8,128)S(1)} %collective-permute-done.27), channel_id=1, source_target_pairs={{0,15},{1,0},{2,1},{3,2},{4,3},{5,4},{6,5},{7,6},{8,7},{9,8},{10,9... | collective-permute-start | bytes 1179656 | tf_op jit(solution)/shard_map/ppermute | solution.py:17
  688.0 13.2 %collective-permute-start.22 = (f32[384,256]{0,1:T(8,128)S(1)}, f32[384,256]{0,1:T(8,128)S(1)}, u32[]{:S(2)}, u32[]{:S(2)}) collective-permute-start(f32[384,256]{0,1:T(8,128)S(1)} %collective-permute-done.21), channel_id=1, source_target_pairs={{0,1},{1,2},{2,3},{3,4},{4,5},{5,6},{6,7},{7,8},{8,9},{9,10},{10,1... | collective-permute-start | bytes 1179656 | tf_op jit(solution)/shard_map/ppermute | solution.py:15
  (16 other events, 609.7 us)
Sparse Core Ops, SparseCore 0:
  44.2 331.0 reduce-scatter.7
  379.8 125.9 reduce-scatter.5
  509.7 179.4 reduce-scatter.3
  731.3 104.0 all-reduce.2
